TPU v7x, 32 devices: a whole 2x2x4 slice. The times are simulated.
32 devices in a mesh: frag: 2 (over y), dev: 4 (over z), col: 4 (over x, core).
Axes of the slice: x: 2, y: 2, z: 4, core: 2. Of those that a mesh axis runs over, the one named last changes fastest.
Arguments:
- factor_ac: bfloat16 [3072, 32, 512], P(('frag', 'dev'), None, 'col'), parts along dimension 0, may hold values from -0.95703125 to 0.95703125
- factor_bd: bfloat16 [3072, 32, 512], P(('frag', 'col'), None, 'dev'), parts along dimension 0, may hold values from -0.95703125 to 0.95703125
- amplitudes: bfloat16 [1024, 512, 256], P(('frag', 'col'), 'dev'), parts along dimension 0, may hold values from -0.015625 to 0.015625
Outputs:
- ladder_residual: float32 [64, 32, 256], P(('frag', 'col'), 'dev'), parts along dimension 0
There are 2 independent parts, one for each index of `frag`. A program takes and returns all parts, laid end to end along the dimension named above; each array names one. Nothing has to cross between parts.
All inputs are finite; a program needn't handle non-finite values.
Results may differ from a plain program's by a relative error of at most 0.0029.
Values may be sent and summed in bfloat16 or wider, within the bound.
A program may use at most 128 MiB of HBM per device.

v0:
```python
import jax
import jax.numpy as jnp
from jax import lax
from jax.sharding import PartitionSpec as P


def local(factor_ac, factor_bd, amplitudes):
    whole_bd = lax.all_gather(factor_bd, "col", axis=0, tiled=True)
    whole_ac = lax.all_gather(factor_ac, "dev", axis=0, tiled=True)
    integral = jnp.einsum("qac,qbd->abdc", whole_ac, whole_bd, preferred_element_type=jnp.float32)
    integral = integral.astype(jnp.bfloat16)
    partial_sum = jnp.einsum(
        "abdc,cdp->abp", integral, amplitudes, preferred_element_type=jnp.float32
    )
    reduced = lax.psum_scatter(partial_sum, "col", scatter_dimension=0, tiled=True)
    result = lax.psum_scatter(reduced, "dev", scatter_dimension=1, tiled=True)
    return result


def solution(mesh):
    placed = (
        P(("frag", "dev"), None, "col"),
        P(("frag", "col"), None, "dev"),
        P(("frag", "col"), "dev", None),
    )
    return jax.shard_map(
        local,
        mesh=mesh,
        in_specs=placed,
        out_specs=P(("frag", "col"), "dev", None),
        check_vma=False,
    )
```

profile of v0, /device:TPU:0, one launch (start us, length us, event | category | flops | bytes accessed | tf_op | source)
XLA Modules:
  0.0 486.6 jit_solution(12520333404982088385)
XLA Ops:
  6.5 0.0 all-gather.5.cloned.1.call-start
  6.5 0.7 all-gather.5.cloned.1.call-update
  7.3 0.0 all-gather.3.cloned.1.call-start
  7.3 0.7 all-gather.3.cloned.1.call-update
  8.0 0.0 reduce-scatter.3.cloned.1.call-start
  8.1 221.8 %all-gather.5.cloned.1.call-done = bf16[1536,32,128]{2,1,0:T(8,128)(2,1)} async-done(((bf16[384,32,128]{2,1,0:T(8,128)(2,1)}), bf16[1536,32,128]{2,1,0:T(8,128)(2,1)}) %all-gather.5.cloned.1.call-update) | async-done | bytes 12582928 | tf_op jit(solution)/shard_map/all_gather | solution.py:9
  229.9 81.9 %all-gather.3.cloned.1.call-done = bf16[1536,32,128]{2,1,0:T(8,128)(2,1)} async-done(((bf16[384,32,128]{2,1,0:T(8,128)(2,1)}), bf16[1536,32,128]{2,1,0:T(8,128)(2,1)}) %all-gather.3.cloned.1.call-update) | async-done | bytes 12582928 | tf_op jit(solution)/shard_map/all_gather | solution.py:8
  311.7 61.4 %fusion.3 = bf16[32,128,32,128]{3,1,2,0:T(8,128)(2,1)} fusion(bf16[1536,32,128,1]{2,1,0,3:T(8,128)(2,1)} %bitcast.15, bf16[1536,32,128,1]{2,1,0,3:T(8,128)(2,1)} %bitcast.16), kind=kOutput, calls=%fused_computation.3 | convolution fusion | flops 51539607552 | bytes 58720256 | tf_op jit(solution)/shard_map/qac,qbd->abdc/dot_general | solution.py:10
  373.1 42.6 %copy.6 = bf16[32,128,32,128]{1,0,3,2:T(8,128)(2,1)} copy(bf16[32,128,32,128]{3,1,2,0:T(8,128)(2,1)} %fusion.3) | data formatting | bytes 67108864 | tf_op jit(solution)/shard_map/qac,qbd->abdc/dot_general | solution.py:10
  415.7 17.4 %fusion.7 = f32[32,32,256]{2,1,0:T(8,128)} fusion(bf16[128,128,256]{2,1,0:T(8,128)(2,1)} %param.5, bf16[32,128,32,128]{1,0,3,2:T(8,128)(2,1)} %copy.6), kind=kOutput, calls=%fused_computation.7 | convolution fusion | flops 8589934592 | bytes 42991616 | tf_op jit(solution)/shard_map/abdc,cdp->abp/dot_general | solution.py:12
  433.1 0.0 reduce-scatter.3.cloned.1.call-update
  433.1 0.0 reduce-scatter.5.cloned.1.call-start
  433.2 25.0 %reduce-scatter.3.cloned.1.call-done = f32[8,32,256]{2,1,0:T(8,128)} async-done(((f32[32,32,256]{2,1,0:T(8,128)}), f32[8,32,256]{2,1,0:T(8,128)}) %reduce-scatter.3.cloned.1.call-update) | async-done | bytes 262160 | tf_op jit(solution)/shard_map/reduce_scatter | solution.py:15
  458.2 0.0 reduce-scatter.5.cloned.1.call-update
  458.2 21.9 %reduce-scatter.5.cloned.1.call-done = f32[8,8,256]{2,1,0:T(8,128)} async-done(((f32[8,32,256]{2,1,0:T(8,128)}), f32[8,8,256]{2,1,0:T(8,128)}) %reduce-scatter.5.cloned.1.call-update) | async-done | bytes 65552 | tf_op jit(solution)/shard_map/reduce_scatter | solution.py:16
Async XLA Ops:
  6.5 223.3 %all-gather.5.cloned.1.call-start = ((), (), s32[]{:S(2)}) async-start(), calls=%async_computation.3 | async-start | bytes 15728640 | tf_op jit(solution)/shard_map/all_gather | solution.py:9
  7.3 304.5 %all-gather.3.cloned.1.call-start = ((), (), s32[]{:S(2)}) async-start(), calls=%async_computation.2 | async-start | bytes 15728640 | tf_op jit(solution)/shard_map/all_gather | solution.py:8
  8.0 450.2 %reduce-scatter.3.cloned.1.call-start = ((), (), s32[]{:S(2)}) async-start(), calls=%async_computation.4 | async-start | bytes 1310720 | tf_op jit(solution)/shard_map/reduce_scatter | solution.py:15
  433.1 46.9 %reduce-scatter.5.cloned.1.call-start = ((), (), s32[]{:S(2)}) async-start(), calls=%async_computation.5 | async-start | bytes 327680 | tf_op jit(solution)/shard_map/reduce_scatter | solution.py:16
Sparse Core Ops, SparseCore 0:
  8.9 220.8 all-gather.4
  231.4 80.2 all-gather.2
  433.2 24.8 reduce-scatter.2
  460.4 19.6 reduce-scatter.4
where the time goes:
time: 488 us; the launch traced here: 487 us
  waiting for transfers between devices  352 us (72%)
  matrix products  78.7 us (16%)
  local copies, waits for them, and re-layouts  42.6 us (9%)
  between operations  13.1 us (3%)
    all_gather x1, waiting for transfers between devices, local(): whole_ac = lax.all_gather(factor_ac, 'dev', axis=0, tiled=True)  222 us
    all_gather x1, waiting for transfers between devices, local(): whole_bd = lax.all_gather(factor_bd, 'col', axis=0, tiled=True)  81.9 us
    dot_general x1, matrix products, local(): jnp.einsum('qac,qbd->abdc', whole_ac, whole_bd, preferred_element_type=jn...  61.4 us
    dot_general x1, local copies, waits for them, and re-layouts, local(): jnp.einsum('qac,qbd->abdc', whole_ac, whole_bd, preferred_element_type=jn...  42.6 us
    reduce_scatter x1, waiting for transfers between devices, local(): lax.psum_scatter(partial_sum, 'col', scatter_dimension=0, tiled=True)  25 us
    reduce_scatter x1, waiting for transfers between devices, local(): result = lax.psum_scatter(reduced, 'dev', scatter_dimension=1, tiled=True)  21.9 us
    dot_general x1, matrix products, local(): jnp.einsum('abdc,cdp->abp', integral, amplitudes, preferred_element_type=...  17.4 us
  transfers between devices with their start and end apart: 4, of which 4 were waited for; matrix products, arithmetic and copies ran while one was open for 0% of the time, Pallas kernels for 0%

commit v1 on v0

v1 whole, which is shorter than its diff:
```python
import functools

import jax
import jax.numpy as jnp
from jax import lax
from jax.experimental import pallas as pl
from jax.experimental.pallas import tpu as pltpu
from jax.sharding import PartitionSpec as P

MESH = pl.DeviceIdType.MESH
CHUNKS = 8
PIECES = 4
AHEAD = 3
NT = 512


def kernel(nz, aw, dw, cw, ac_ref, bd_ref, t_ref, out_ref, ac_all, bd_all, t_all, x_buf,
           load_sem, bd_send, bd_recv, fw_send, fw_recv, send_r, recv_r, send_l, recv_l):
    z = lax.axis_index("dev")
    me = lax.axis_index("col")
    sib = me + 1 - 2 * lax.rem(me, 2)
    far = lax.rem(me + 2, 4)
    farsib = lax.rem(sib + 2, 4)
    has_r, has_l = z < nz - 1, z > 0
    rows_total, qz = ac_ref.shape
    qc, n_total = bd_ref.shape
    rows = rows_total // CHUNKS
    part = qc // PIECES
    hops = nz - 1

    barrier = pltpu.get_barrier_semaphore()
    for peer in (sib, far):
        pl.semaphore_signal(barrier, inc=1, device_id={"col": peer}, device_id_type=MESH)

    @pl.when(has_r)
    def _():
        pl.semaphore_signal(barrier, inc=1, device_id={"dev": z + 1}, device_id_type=MESH)

    @pl.when(has_l)
    def _():
        pl.semaphore_signal(barrier, inc=1, device_id={"dev": z - 1}, device_id_type=MESH)

    pl.semaphore_wait(barrier, 2 + has_r.astype(jnp.int32) + has_l.astype(jnp.int32))

    def ac_slot(j, k):
        return ac_all.at[pl.ds(pl.multiple_of(k * rows, rows), rows),
                         pl.ds(pl.multiple_of(j * qz, qz), qz)]

    def own(k):
        return ac_ref.at[pl.ds(pl.multiple_of(k * rows, rows), rows), :]

    def right(h, k):
        j = z - h
        return pltpu.make_async_remote_copy(
            src_ref=own(k) if h == 0 else ac_slot(j, k), dst_ref=ac_slot(j, k),
            send_sem=send_r.at[h, k], recv_sem=recv_r.at[h, k],
            device_id={"dev": z + 1}, device_id_type=MESH)

    def left(h, k):
        j = z + h
        return pltpu.make_async_remote_copy(
            src_ref=own(k) if h == 0 else ac_slot(j, k), dst_ref=ac_slot(j, k),
            send_sem=send_l.at[h, k], recv_sem=recv_l.at[h, k],
            device_id={"dev": z - 1}, device_id_type=MESH)

    def from_left(h, k):
        j = z - 1 - h
        return pltpu.make_async_remote_copy(
            src_ref=ac_slot(j, k), dst_ref=ac_slot(j, k),
            send_sem=send_r.at[h, k], recv_sem=recv_r.at[h, k],
            device_id={"dev": z - 1}, device_id_type=MESH)

    def from_right(h, k):
        j = z + 1 + h
        return pltpu.make_async_remote_copy(
            src_ref=ac_slot(j, k), dst_ref=ac_slot(j, k),
            send_sem=send_l.at[h, k], recv_sem=recv_l.at[h, k],
            device_id={"dev": z + 1}, device_id_type=MESH)

    def send_own(k):
        @pl.when(has_r)
        def _():
            right(0, k).start()

        @pl.when(has_l)
        def _():
            left(0, k).start()

    def bd_slot(j, p):
        return bd_all.at[pl.ds(pl.multiple_of(j * qc + p * part, part), part), :]

    def bd_own(p):
        return bd_ref.at[pl.ds(p * part, part), :]

    def bd_copy(way, j, p, peer, own_src):
        ss, rs = (fw_send, fw_recv) if way == 2 else (bd_send.at[way], bd_recv.at[way])
        return pltpu.make_async_remote_copy(
            src_ref=bd_own(p) if own_src else bd_slot(j, p), dst_ref=bd_slot(j, p),
            send_sem=ss.at[p], recv_sem=rs.at[p],
            device_id={"col": peer}, device_id_type=MESH)

    for p in range(PIECES):
        bd_copy(0, me, p, far, True).start()
    for k in range(AHEAD):
        send_own(k)
    for p in range(PIECES):
        bd_copy(1, me, p, sib, True).start()
    loads = [
        pltpu.make_async_copy(bd_ref, bd_all.at[pl.ds(pl.multiple_of(me * qc, qc), qc), :], load_sem.at[0]),
        pltpu.make_async_copy(ac_ref, ac_all.at[:, pl.ds(pl.multiple_of(z * qz, qz), qz)], load_sem.at[1]),
        pltpu.make_async_copy(t_ref, t_all, load_sem.at[2]),
    ]
    for copy in loads:
        copy.start()
    out_ref[...] = jnp.zeros_like(out_ref)

    def pump(h, k):
        @pl.when(z - 1 - h >= 0)
        def _():
            from_left(h, k).wait_recv()
            if h + 1 < hops:
                @pl.when(has_r)
                def _():
                    right(h + 1, k).start()

        @pl.when(z + 1 + h < nz)
        def _():
            from_right(h, k).wait_recv()
            if h + 1 < hops:
                @pl.when(has_l)
                def _():
                    left(h + 1, k).start()

    def compute(k):
        first = pl.multiple_of(k * rows, rows)
        c_in = rows // aw
        b_in = NT // dw

        def tile(n, carry):
            block = jnp.dot(
                ac_all[pl.ds(first, rows), :],
                bd_all[:, pl.ds(pl.multiple_of(n * NT, NT), NT)],
                preferred_element_type=jnp.float32,
            ).astype(jnp.bfloat16)
            for b in range(b_in):
                at = pl.multiple_of((n * b_in + b) * aw, aw)
                for c in range(c_in):
                    x_buf[pl.ds(at, aw), c * dw:(c + 1) * dw] = (
                        block[c * aw:(c + 1) * aw, b * dw:(b + 1) * dw])
            return carry

        lax.fori_loop(0, n_total // NT, tile, 0)
        kk = c_in * dw
        m = 256

        def add(i, carry):
            at = pl.ds(pl.multiple_of(i * m, m), m)
            out_ref[at, :] += jnp.dot(
                x_buf[at, :], t_all[pl.ds(pl.multiple_of(k * kk, kk), kk), :],
                preferred_element_type=jnp.float32)
            return carry

        lax.fori_loop(0, out_ref.shape[0] // m, add, 0)

    def step(s, carry):
        @pl.when(s + AHEAD < CHUNKS)
        def _():
            send_own(s + AHEAD)

        for h in range(hops):
            @pl.when((s >= h) & (s - h < CHUNKS))
            def _():
                pump(h, s - h)

        @pl.when(s == hops - 1)
        def _():
            for p in range(PIECES):
                bd_copy(0, far, p, far, False).wait_recv()
                bd_copy(2, far, p, sib, False).start()
            for p in range(PIECES):
                bd_copy(1, sib, p, sib, False).wait_recv()
            for p in range(PIECES):
                bd_copy(2, farsib, p, sib, False).wait_recv()
            for copy in loads:
                copy.wait()

        @pl.when(s >= hops - 1)
        def _():
            compute(s - (hops - 1))

        return carry

    lax.fori_loop(0, CHUNKS + hops - 1, step, 0)

    for p in range(PIECES):
        bd_copy(0, me, p, far, True).wait_send()
        bd_copy(1, me, p, sib, True).wait_send()
        bd_copy(2, far, p, sib, False).wait_send()

    def drain(k, carry):
        for h in range(hops):
            @pl.when(has_r & (z - h >= 0))
            def _():
                right(h, k).wait_send()

            @pl.when(has_l & (z + h < nz))
            def _():
                left(h, k).wait_send()
        return carry

    lax.fori_loop(0, CHUNKS, drain, 0)


def fused(nz, factor_ac, factor_bd, amplitudes):
    qz, aw, cw = factor_ac.shape
    qc, bw, dw = factor_bd.shape
    npair = amplitudes.shape[2]
    rows_ac = factor_ac.transpose(2, 1, 0).reshape(cw * aw, qz)
    rows_bd = factor_bd.reshape(qc, bw * dw)
    rows_t = amplitudes.reshape(cw * dw, npair)
    hops = nz - 1
    dma = pltpu.SemaphoreType.DMA
    any_space = pl.BlockSpec(memory_space=pl.ANY)
    partial_sum = pl.pallas_call(
        functools.partial(kernel, nz, aw, dw, cw),
        out_shape=jax.ShapeDtypeStruct((bw * aw, npair), jnp.float32),
        in_specs=[any_space] * 3,
        out_specs=pl.BlockSpec(memory_space=pltpu.VMEM),
        scratch_shapes=[
            pltpu.VMEM((cw * aw, nz * qz), jnp.bfloat16),
            pltpu.VMEM((4 * qc, bw * dw), jnp.bfloat16),
            pltpu.VMEM((cw * dw, npair), jnp.bfloat16),
            pltpu.VMEM((bw * aw, cw // CHUNKS * dw), jnp.bfloat16),
            dma((3,)), dma((2, PIECES)), dma((2, PIECES)), dma((PIECES,)), dma((PIECES,)),
            dma((hops, CHUNKS)), dma((hops, CHUNKS)), dma((hops, CHUNKS)), dma((hops, CHUNKS)),
        ],
        compiler_params=pltpu.CompilerParams(
            collective_id=0, has_side_effects=True, vmem_limit_bytes=58 * 2 ** 20),
    )(rows_ac, rows_bd, rows_t)
    partial_sum = partial_sum.reshape(bw, aw, npair)
    reduced = lax.psum_scatter(partial_sum, "col", scatter_dimension=1, tiled=True)
    result = lax.psum_scatter(reduced, "dev", scatter_dimension=0, tiled=True)
    return result.transpose(1, 0, 2)


def gathered(factor_ac, factor_bd, amplitudes):
    whole_bd = lax.all_gather(factor_bd, "col", axis=0, tiled=True)
    whole_ac = lax.all_gather(factor_ac, "dev", axis=0, tiled=True)
    integral = jnp.einsum("qac,qbd->abdc", whole_ac, whole_bd, preferred_element_type=jnp.float32)
    integral = integral.astype(jnp.bfloat16)
    partial_sum = jnp.einsum(
        "abdc,cdp->abp", integral, amplitudes, preferred_element_type=jnp.float32
    )
    reduced = lax.psum_scatter(partial_sum, "col", scatter_dimension=0, tiled=True)
    return lax.psum_scatter(reduced, "dev", scatter_dimension=1, tiled=True)


def solution(mesh):
    nz, ncol = mesh.shape["dev"], mesh.shape["col"]

    def local(factor_ac, factor_bd, amplitudes):
        qz, aw, cw = factor_ac.shape
        qc, bw, dw = factor_bd.shape
        held = 2 * (cw * aw * nz * qz + ncol * qc * bw * dw + cw * dw * amplitudes.shape[2])
        fits = (ncol == 4 and 2 <= nz and dw == 128 and qz % 128 == 0 and qc % (16 * PIECES) == 0
                and aw % 16 == 0 and cw % CHUNKS == 0 and bw * dw % NT == 0
                and bw * aw % 256 == 0 and CHUNKS >= AHEAD and held <= 36 * 2 ** 20)
        if fits:
            return fused(nz, factor_ac, factor_bd, amplitudes)
        return gathered(factor_ac, factor_bd, amplitudes)

    placed = (
        P(("frag", "dev"), None, "col"),
        P(("frag", "col"), None, "dev"),
        P(("frag", "col"), "dev", None),
    )
    return jax.shard_map(
        local,
        mesh=mesh,
        in_specs=placed,
        out_specs=P(("frag", "col"), "dev", None),
        check_vma=False,
    )
```

time: 488 us -> 295 us (0.60)
  waiting for transfers between devices: 352 us -> 47.2 us
  Pallas kernels: 0 us -> 223 us
  matrix products: 78.7 us -> 0 us
  local copies, waits for them, and re-layouts: 42.6 us -> 11.6 us
    all_gather x2 -> x0, waiting for transfers between devices: 304 us -> none  [the longest x1 222 us: local(): whole_ac = lax.all_gather(factor_ac, 'dev', axis=0, tiled=True)]
    pallas_call x0 -> x1, Pallas kernels: none -> 223 us  [fused(): pl.pallas_call(functools.partial(kernel, nz, aw, dw, cw), out_shape=jax.S...]
    dot_general x2 -> x0, matrix products: 78.7 us -> none  [the longest x1 61.4 us: local(): jnp.einsum('qac,qbd->abdc', whole_ac, whole_bd, preferred_element_type=jn...]
    dot_general x1 -> x0, local copies, waits for them, and re-layouts: 42.6 us -> none  [local(): jnp.einsum('qac,qbd->abdc', whole_ac, whole_bd, preferred_element_type=jn...]
    transpose x0 -> x1, local copies, waits for them, and re-layouts: none -> 5.62 us  [fused(): rows_ac = factor_ac.transpose(2, 1, 0).reshape(cw * aw, qz)]
  transfers between devices with their start and end apart: 4 -> 2, of which waited for: 4 -> 2; matrix products, arithmetic and copies ran while one was open for 0% -> 0% of each run, Pallas kernels for 0% -> 0%
where the time goes in v1:
time: 295 us
  Pallas kernels  223 us (76%)
  waiting for transfers between devices  47.2 us (16%)
  between operations  13.4 us (5%)
  local copies, waits for them, and re-layouts  11.6 us (4%)
    pallas_call x1, Pallas kernels, fused(): pl.pallas_call(functools.partial(kernel, nz, aw, dw, cw), out_shape=jax.S...  223 us
    reduce_scatter x1, waiting for transfers between devices, fused(): lax.psum_scatter(partial_sum, 'col', scatter_dimension=1, tiled=True)  25.1 us
    reduce_scatter x1, waiting for transfers between devices, fused(): result = lax.psum_scatter(reduced, 'dev', scatter_dimension=0, tiled=True)  22 us
  transfers between devices with their start and end apart: 2, of which 2 were waited for; matrix products, arithmetic and copies ran while one was open for 0% of the time, Pallas kernels for 0%

profile of v1, /device:TPU:0, one launch (start us, length us, event | category | flops | bytes accessed | tf_op | source)
XLA Modules:
  0.0 294.8 jit_solution(9613182771007735104)
XLA Ops:
  6.5 0.0 reduce-scatter.3.cloned.1.call-start
  6.5 0.0 copy-start
  6.5 5.6 %copy.4 = bf16[128,32,384]{2,1,0:T(8,128)(2,1)} copy(bf16[128,32,384]{0,1,2:T(8,128)(2,1)} %bitcast.13) | data formatting | bytes 6291456 | tf_op jit(solution)/shard_map/transpose | solution.py:218
  12.2 0.0 copy-done
  12.2 3.2 %copy.8 = bf16[48,8,32,128]{3,1,2,0:T(8,128)(2,1)} copy(bf16[48,8,32,128]{3,2,1,0:T(8,128)(2,1)S(1)} %bitcast.14) | data formatting | bytes 6291456
  15.4 222.6 %shard_map.37 = f32[1024,256]{1,0:T(8,128)} custom-call(bf16[4096,384]{1,0:T(8,128)(2,1)} %bitcast.9, bf16[384,4096]{1,0:T(8,128)(2,1)} %bitcast.10, bf16[16384,256]{1,0:T(8,128)(2,1)} %bitcast.11), custom_call_target="tpu_custom_call" | custom-call | tf_op jit(solution)/shard_map/pallas_call | solution.py:224
  238.0 2.8 copy.5
  240.8 0.0 reduce-scatter.3.cloned.1.call-update
  240.8 0.0 reduce-scatter.5.cloned.1.call-start
  240.8 25.1 %reduce-scatter.3.cloned.1.call-done = f32[32,8,256]{2,0,1:T(8,128)} async-done(((f32[32,32,256]{2,0,1:T(8,128)}), f32[32,8,256]{2,0,1:T(8,128)}) %reduce-scatter.3.cloned.1.call-update) | async-done | bytes 262160 | tf_op jit(solution)/shard_map/reduce_scatter | solution.py:241
  266.0 0.0 reduce-scatter.5.cloned.1.call-update
  266.0 22.0 %reduce-scatter.5.cloned.1.call-done = f32[8,8,256]{2,0,1:T(8,128)} async-done(((f32[32,8,256]{2,0,1:T(8,128)}), f32[8,8,256]{2,0,1:T(8,128)}) %reduce-scatter.5.cloned.1.call-update) | async-done | bytes 65552 | tf_op jit(solution)/shard_map/reduce_scatter | solution.py:242
Async XLA Ops:
  6.5 259.4 %reduce-scatter.3.cloned.1.call-start = ((), (), s32[]{:S(2)}) async-start(), calls=%async_computation.2 | async-start | bytes 1310720 | tf_op jit(solution)/shard_map/reduce_scatter | solution.py:241
  6.5 5.6 %copy-start = (bf16[384,32,128]{2,1,0:T(8,128)(2,1)S(1)}, bf16[384,32,128]{2,1,0:T(8,128)(2,1)}, u32[]{:S(2)}) copy-start(bf16[384,32,128]{2,1,0:T(8,128)(2,1)} %param.4) | copy-start | bytes 9437188
  240.8 47.2 %reduce-scatter.5.cloned.1.call-start = ((), (), s32[]{:S(2)}) async-start(), calls=%async_computation.3 | async-start | bytes 327680 | tf_op jit(solution)/shard_map/reduce_scatter | solution.py:242
Sparse Core Ops, SparseCore 0:
  240.9 24.9 reduce-scatter.2
  268.3 19.6 reduce-scatter.4

commit v2 on v1

--- a/solution.py
+++ b/solution.py
@@ -237,10 +237,9 @@
         compiler_params=pltpu.CompilerParams(
             collective_id=0, has_side_effects=True, vmem_limit_bytes=58 * 2 ** 20),
     )(rows_ac, rows_bd, rows_t)
-    partial_sum = partial_sum.reshape(bw, aw, npair)
-    reduced = lax.psum_scatter(partial_sum, "col", scatter_dimension=1, tiled=True)
-    result = lax.psum_scatter(reduced, "dev", scatter_dimension=0, tiled=True)
-    return result.transpose(1, 0, 2)
+    blocks = partial_sum.reshape(nz, bw // nz, 4, aw // 4, npair).transpose(2, 0, 3, 1, 4)
+    blocks = blocks.reshape(4 * nz, aw // 4, bw // nz, npair)
+    return lax.all_to_all(blocks, ("col", "dev"), 0, 0, tiled=True).sum(0)
 
 
 def gathered(factor_ac, factor_bd, amplitudes):
@@ -263,7 +262,7 @@
         qc, bw, dw = factor_bd.shape
         held = 2 * (cw * aw * nz * qz + ncol * qc * bw * dw + cw * dw * amplitudes.shape[2])
         fits = (ncol == 4 and 2 <= nz and dw == 128 and qz % 128 == 0 and qc % (16 * PIECES) == 0
-                and aw % 16 == 0 and cw % CHUNKS == 0 and bw * dw % NT == 0
+                and aw % 16 == 0 and bw % nz == 0 and cw % CHUNKS == 0 and bw * dw % NT == 0
                 and bw * aw % 256 == 0 and CHUNKS >= AHEAD and held <= 36 * 2 ** 20)
         if fits:
             return fused(nz, factor_ac, factor_bd, amplitudes)

time: 295 us -> 266 us (0.902)
  waiting for transfers between devices: 47.2 us -> 0 us
  blocking collectives: 0 us -> 31.5 us
  between operations: 13.4 us -> 0.01 us
    reduce_scatter x2 -> x0, waiting for transfers between devices: 47.1 us -> none  [the longest x1 25.1 us: fused(): lax.psum_scatter(partial_sum, 'col', scatter_dimension=1, tiled=True)]
    all_to_all x0 -> x1, blocking collectives: none -> 31.5 us  [fused(): return lax.all_to_all(blocks, ('col', 'dev'), 0, 0, tiled=True).sum(0)]
  transfers between devices with their start and end apart: 2 -> 0, of which waited for: 2 -> 0; matrix products, arithmetic and copies ran while one was open for 0% -> 0% of each run, Pallas kernels for 0% -> 0%
where the time goes in v2:
time: 266 us
  Pallas kernels  223 us (84%)
  blocking collectives  31.5 us (12%)
  local copies, waits for them, and re-layouts  10.7 us (4%)
    pallas_call x1, Pallas kernels, fused(): pl.pallas_call(functools.partial(kernel, nz, aw, dw, cw), out_shape=jax.S...  223 us
    all_to_all x1, blocking collectives, fused(): return lax.all_to_all(blocks, ('col', 'dev'), 0, 0, tiled=True).sum(0)  31.5 us
    transpose x1, local copies, waits for them, and re-layouts, fused(): rows_ac = factor_ac.transpose(2, 1, 0).reshape(cw * aw, qz)  5.64 us

profile of v2, /device:TPU:0, one launch (start us, length us, event | category | flops | bytes accessed | tf_op | source)
XLA Modules:
  0.0 265.5 jit_solution(2755894366786871198)
XLA Ops:
  0.0 0.0 copy-start
  0.0 5.6 %copy.5 = bf16[128,32,384]{2,1,0:T(8,128)(2,1)} copy(bf16[128,32,384]{0,1,2:T(8,128)(2,1)} %bitcast.16) | data formatting | bytes 6291456 | tf_op jit(solution)/shard_map/transpose | solution.py:218
  5.6 0.0 copy-done
  5.6 3.2 %copy.9 = bf16[48,8,32,128]{3,1,2,0:T(8,128)(2,1)} copy(bf16[48,8,32,128]{3,2,1,0:T(8,128)(2,1)S(1)} %bitcast.17) | data formatting | bytes 6291456
  8.9 222.6 %shard_map.37 = f32[1024,256]{1,0:T(8,128)} custom-call(bf16[4096,384]{1,0:T(8,128)(2,1)} %bitcast.11, bf16[384,4096]{1,0:T(8,128)(2,1)} %bitcast.12, bf16[16384,256]{1,0:T(8,128)(2,1)} %bitcast.13), custom_call_target="tpu_custom_call" | custom-call | tf_op jit(solution)/shard_map/pallas_call | solution.py:224
  231.5 1.8 copy.6
  233.3 31.5 %all_to_all.5 = f32[16,8,8,256]{3,2,1,0:T(8,128)S(1)} all-to-all(f32[16,8,8,256]{3,2,1,0:T(8,128)S(1)} %bitcast.14), channel_id=1, replica_groups=mesh['frag'=2,'dev'=4,'col'=4] {'col','dev'}, dimensions={0} | all-to-all | bytes 2097152 | tf_op jit(solution)/shard_map/all_to_all | solution.py:242
  264.8 0.7 reduce_sum.9
Async XLA Ops:
  0.0 5.6 %copy-start = (bf16[384,32,128]{2,1,0:T(8,128)(2,1)S(1)}, bf16[384,32,128]{2,1,0:T(8,128)(2,1)}, u32[]{:S(2)}) copy-start(bf16[384,32,128]{2,1,0:T(8,128)(2,1)} %param.4) | copy-start | bytes 9437188

commit v3 on v1

--- a/solution.py
+++ b/solution.py
@@ -11,10 +11,10 @@
 CHUNKS = 8
 PIECES = 4
 AHEAD = 3
-NT = 512
-
-
-def kernel(nz, aw, dw, cw, ac_ref, bd_ref, t_ref, out_ref, ac_all, bd_all, t_all, x_buf,
+NT = 1024
+
+
+def kernel(nz, aw, dw, cw, ac_ref, bd_ref, t_ref, out_ref, ac_all, bd_all, t_all, x_buf, total,
            load_sem, bd_send, bd_recv, fw_send, fw_recv, send_r, recv_r, send_l, recv_l):
     z = lax.axis_index("dev")
     me = lax.axis_index("col")
@@ -112,7 +112,7 @@
     ]
     for copy in loads:
         copy.start()
-    out_ref[...] = jnp.zeros_like(out_ref)
+    total[...] = jnp.zeros_like(total)
 
     def pump(h, k):
         @pl.when(z - 1 - h >= 0)
@@ -155,12 +155,12 @@
 
         def add(i, carry):
             at = pl.ds(pl.multiple_of(i * m, m), m)
-            out_ref[at, :] += jnp.dot(
+            total[at, :] += jnp.dot(
                 x_buf[at, :], t_all[pl.ds(pl.multiple_of(k * kk, kk), kk), :],
                 preferred_element_type=jnp.float32)
             return carry
 
-        lax.fori_loop(0, out_ref.shape[0] // m, add, 0)
+        lax.fori_loop(0, total.shape[0] // m, add, 0)
 
     def step(s, carry):
         @pl.when(s + AHEAD < CHUNKS)
@@ -191,6 +191,17 @@
         return carry
 
     lax.fori_loop(0, CHUNKS + hops - 1, step, 0)
+
+    a_own = aw // 4
+    bw = n_total // dw
+
+    def place(b, carry):
+        for a in range(4):
+            out_ref[pl.ds(pl.multiple_of((a * bw + b) * a_own, a_own), a_own), :] = (
+                total[pl.ds(pl.multiple_of(b * aw + a * a_own, a_own), a_own), :])
+        return carry
+
+    lax.fori_loop(0, bw, place, 0)
 
     for p in range(PIECES):
         bd_copy(0, me, p, far, True).wait_send()
@@ -231,15 +242,15 @@
             pltpu.VMEM((4 * qc, bw * dw), jnp.bfloat16),
             pltpu.VMEM((cw * dw, npair), jnp.bfloat16),
             pltpu.VMEM((bw * aw, cw // CHUNKS * dw), jnp.bfloat16),
+            pltpu.VMEM((bw * aw, npair), jnp.float32),
             dma((3,)), dma((2, PIECES)), dma((2, PIECES)), dma((PIECES,)), dma((PIECES,)),
             dma((hops, CHUNKS)), dma((hops, CHUNKS)), dma((hops, CHUNKS)), dma((hops, CHUNKS)),
         ],
         compiler_params=pltpu.CompilerParams(
             collective_id=0, has_side_effects=True, vmem_limit_bytes=58 * 2 ** 20),
     )(rows_ac, rows_bd, rows_t)
-    partial_sum = partial_sum.reshape(bw, aw, npair)
-    reduced = lax.psum_scatter(partial_sum, "col", scatter_dimension=1, tiled=True)
-    result = lax.psum_scatter(reduced, "dev", scatter_dimension=0, tiled=True)
+    blocks = partial_sum.reshape(4 * nz, bw // nz, aw // 4, npair)
+    result = lax.all_to_all(blocks, ("col", "dev"), 0, 0, tiled=True).sum(0)
     return result.transpose(1, 0, 2)
 
 
@@ -263,7 +274,7 @@
         qc, bw, dw = factor_bd.shape
         held = 2 * (cw * aw * nz * qz + ncol * qc * bw * dw + cw * dw * amplitudes.shape[2])
         fits = (ncol == 4 and 2 <= nz and dw == 128 and qz % 128 == 0 and qc % (16 * PIECES) == 0
-                and aw % 16 == 0 and cw % CHUNKS == 0 and bw * dw % NT == 0
+                and aw % 32 == 0 and bw % nz == 0 and cw % CHUNKS == 0 and bw * dw % NT == 0
                 and bw * aw % 256 == 0 and CHUNKS >= AHEAD and held <= 36 * 2 ** 20)
         if fits:
             return fused(nz, factor_ac, factor_bd, amplitudes)

time: 295 us -> 263 us (0.89)
  waiting for transfers between devices: 47.2 us -> 0 us
  blocking collectives: 0 us -> 31.7 us
  between operations: 13.4 us -> 0.01 us
    reduce_scatter x2 -> x0, waiting for transfers between devices: 47.1 us -> none  [the longest x1 25.1 us: fused(): lax.psum_scatter(partial_sum, 'col', scatter_dimension=1, tiled=True)]
    all_to_all x0 -> x1, blocking collectives: none -> 31.7 us  [fused(): result = lax.all_to_all(blocks, ('col', 'dev'), 0, 0, tiled=True).sum(0)]
  transfers between devices with their start and end apart: 2 -> 0, of which waited for: 2 -> 0; matrix products, arithmetic and copies ran while one was open for 0% -> 0% of each run, Pallas kernels for 0% -> 0%
where the time goes in v3:
time: 263 us
  Pallas kernels  222 us (84%)
  blocking collectives  31.7 us (12%)
  local copies, waits for them, and re-layouts  9.52 us (4%)
    pallas_call x1, Pallas kernels, fused(): pl.pallas_call(functools.partial(kernel, nz, aw, dw, cw), out_shape=jax.S...  222 us
    all_to_all x1, blocking collectives, fused(): result = lax.all_to_all(blocks, ('col', 'dev'), 0, 0, tiled=True).sum(0)  31.7 us
    transpose x1, local copies, waits for them, and re-layouts, fused(): rows_ac = factor_ac.transpose(2, 1, 0).reshape(cw * aw, qz)  5.64 us

profile of v3, /device:TPU:0, one launch (start us, length us, event | category | flops | bytes accessed | tf_op | source)
XLA Modules:
  0.0 263.1 jit_solution(7230928397107726759)
XLA Ops:
  0.0 0.0 copy-start
  0.0 5.6 %copy.5 = bf16[128,32,384]{2,1,0:T(8,128)(2,1)} copy(bf16[128,32,384]{0,1,2:T(8,128)(2,1)} %bitcast.13) | data formatting | bytes 6291456 | tf_op jit(solution)/shard_map/transpose | solution.py:229
  5.6 0.0 copy-done
  5.6 3.2 %copy.9 = bf16[48,8,32,128]{3,1,2,0:T(8,128)(2,1)} copy(bf16[48,8,32,128]{3,2,1,0:T(8,128)(2,1)S(1)} %bitcast.14) | data formatting | bytes 6291456
  8.9 221.8 %shard_map.37 = f32[1024,256]{1,0:T(8,128)} custom-call(bf16[4096,384]{1,0:T(8,128)(2,1)} %bitcast.9, bf16[384,4096]{1,0:T(8,128)(2,1)} %bitcast.10, bf16[16384,256]{1,0:T(8,128)(2,1)} %bitcast.11), custom_call_target="tpu_custom_call" | custom-call | tf_op jit(solution)/shard_map/pallas_call | solution.py:235
  230.6 31.7 %all_to_all.5 = f32[16,8,8,256]{3,2,1,0:T(8,128)S(1)} all-to-all(f32[16,8,8,256]{3,2,1,0:T(8,128)} %bitcast.12), channel_id=1, replica_groups=mesh['frag'=2,'dev'=4,'col'=4] {'col','dev'}, dimensions={0} | all-to-all | bytes 2097152 | tf_op jit(solution)/shard_map/all_to_all | solution.py:253
  262.4 0.1 reduce_sum.9
  262.4 0.7 copy.6
Async XLA Ops:
  0.0 5.6 %copy-start = (bf16[384,32,128]{2,1,0:T(8,128)(2,1)S(1)}, bf16[384,32,128]{2,1,0:T(8,128)(2,1)}, u32[]{:S(2)}) copy-start(bf16[384,32,128]{2,1,0:T(8,128)(2,1)} %param.4) | copy-start | bytes 9437188
